TPU v7x, 32 devices: a whole 2x2x4 slice. The times are simulated.
32 devices in a mesh: row: 4 (over y, core), col: 8 (over z, x).
Axes of the slice: x: 2, y: 2, z: 4, core: 2. Of those that a mesh axis runs over, the one named last changes fastest.
Arguments:
- volts: bfloat16 [2, 512, 4096], P(None, ('row', 'col')), may hold values from -6 to 6
- pattern: int32 [32, 32], replicated, may hold values from -1 to 62, as said below
- owner_slot: int32 [64], replicated, may hold values from 0 to 63, each once
Outputs:
- stacks: float32 [64, 4, 255], P(('row', 'col'))
Inputs may be any that keep to these rules, and one draw needn't show every extreme that they name: pattern[p, q] is either q - p + 31 or -1; it is -1 where p == q. `owner_slot`: a permutation.
All inputs are finite; a program needn't handle non-finite values.
Results may differ from a plain program's by a relative error of at most 0.0003.
Values may be sent and summed in bfloat16 or wider, within the bound.
A program may use at most 64 MiB of HBM per device.

v0:
```python
import jax
import jax.numpy as jnp
from jax import lax
from jax.sharding import PartitionSpec as P

GRID_COLUMNS = 128
RPD = 1
CHAN = 2
TIME_SAMPLES = 256


def per_device(volts, pattern, owner_slot):
    row_count = lax.axis_size("row")
    col_count = lax.axis_size("col")
    device_count = row_count * col_count
    stack_count = owner_slot.shape[0]
    sep_count = 2 * GRID_COLUMNS - 1
    lane_width = 2 * GRID_COLUMNS
    grid_rows = pattern.shape[0]
    turned = lax.all_to_all(volts, ("row", "col"), split_axis=2, concat_axis=1, tiled=True)
    local_volts = turned.reshape(2, CHAN, TIME_SAMPLES, turned.shape[2])
    column_side = lax.all_gather(local_volts, "row", axis=3, tiled=True)
    pair_cols = column_side.shape[3] // GRID_COLUMNS
    column_side = column_side.reshape(2, CHAN, TIME_SAMPLES, pair_cols, GRID_COLUMNS)
    column_rot = jnp.stack([-column_side[1], column_side[0]])
    row_index = lax.axis_index("row")
    col_index = lax.axis_index("col")
    row_rows = RPD * col_count
    pattern_rows = lax.dynamic_slice_in_dim(pattern, row_index * row_rows, row_rows, 0)
    pattern_rows = pattern_rows.reshape(row_rows, row_count, col_count, RPD)
    selected = lax.dynamic_index_in_dim(pattern_rows, col_index, 2, keepdims=False)
    selected = selected.reshape(row_rows, pair_cols)
    stack_ids = jnp.arange(stack_count, dtype=jnp.int32)
    first_col = jnp.arange(GRID_COLUMNS, dtype=jnp.int32)[:, None, None]
    second_col = jnp.arange(GRID_COLUMNS, dtype=jnp.int32)[None, :, None]
    separation = jnp.arange(lane_width, dtype=jnp.int32)[None, None, :]
    fold_table = (second_col - first_col + GRID_COLUMNS - 1 == separation).astype(jnp.float32)
    highest = lax.Precision.HIGHEST
    initial = jnp.zeros((col_count, stack_count // col_count, 2 * CHAN, lane_width), jnp.float32)
    piece = lax.all_gather(local_volts, "col", axis=3, tiled=True)
    row_total = piece.shape[3] // GRID_COLUMNS

    def one_row(offset, running):
        current = lax.dynamic_slice_in_dim(piece, offset * GRID_COLUMNS, GRID_COLUMNS, 3)
        real_part = jnp.einsum(
            "xcta,xctqb->qcab", current, column_side, preferred_element_type=jnp.float32
        )
        imag_part = jnp.einsum(
            "xcta,xctqb->qcab", current, column_rot, preferred_element_type=jnp.float32
        )
        gram = jnp.stack([real_part, imag_part], axis=2)
        folded = jnp.einsum("qcpab,abs->qcps", gram, fold_table, precision=highest)
        folded = folded.reshape(1, pair_cols, 2 * CHAN, lane_width)
        keys = lax.dynamic_index_in_dim(selected, offset, 0, keepdims=False)
        grid_row = row_index * row_rows + offset
        lowest = col_index - grid_row + grid_rows - 1
        block_start = lowest // col_count
        lane = lowest % col_count
        zero = jnp.zeros((), jnp.int32)
        corner = (lane, block_start, zero, zero)
        window = lax.dynamic_slice(running, corner, (1, pair_cols, 2 * CHAN, lane_width))
        window = window + jnp.where((keys >= 0)[None, :, None, None], folded, 0.0)
        return lax.dynamic_update_slice(running, window, corner)

    by_lane = lax.fori_loop(0, row_total, one_row, initial)
    by_stack = by_lane.transpose(1, 0, 2, 3).reshape(stack_count, 2 * CHAN, lane_width)
    by_stack = by_stack[:, :, :sep_count]
    inverse = jnp.zeros((stack_count,), jnp.int32).at[owner_slot].set(stack_ids)
    partial_sums = jnp.take(by_stack, inverse, axis=0)
    slot_count = stack_count // device_count
    owned = lax.psum_scatter(partial_sums, ("row", "col"), scatter_dimension=0, tiled=True)
    device_index = lax.axis_index(("row", "col"))
    key_of = lax.dynamic_slice_in_dim(inverse, device_index * slot_count, slot_count, 0)
    pair_counts = jnp.sum(
        (pattern[None, :, :] == key_of[:, None, None]).astype(jnp.float32), axis=(1, 2)
    )
    separation_offsets = jnp.abs(jnp.arange(sep_count, dtype=jnp.float32) - (GRID_COLUMNS - 1.0))
    antenna_pairs = pair_counts[:, None] * (GRID_COLUMNS - separation_offsets)[None, :]
    stack_scale = 1.0 / jnp.sqrt(2.0 * TIME_SAMPLES * jnp.maximum(antenna_pairs, 1.0))
    return owned * stack_scale[:, None, :]


def solution(mesh):
    return jax.shard_map(
        per_device,
        mesh=mesh,
        in_specs=(P(None, ("row", "col"), None), P(), P()),
        out_specs=P(("row", "col"), None, None),
        check_vma=False,
    )
```

profile of v0, /device:TPU:0, one launch (start us, length us, event | category | flops | bytes accessed | tf_op | source)
XLA Modules:
  0.0 337.6 jit_solution(12674714906885499957)
XLA Ops:
  6.5 4.5 %copy.45 = bf16[2,16,4096]{1,0,2:T(2,128)(2,1)S(1)} copy(bf16[2,16,4096]{2,1,0:T(8,128)(2,1)} %param.5) | data formatting | bytes 524288 | tf_op args[0]
  11.0 2.2 reshape.166
  13.3 17.8 %all_to_all.15 = bf16[32,2,2048]{2,1,0:T(2,128)(2,1)S(1)} all-to-all(bf16[32,2,2048]{2,1,0:T(2,128)(2,1)S(1)} %reshape.166), channel_id=1, replica_groups=mesh['row'=4,'col'=8] {'row','col'}, dimensions={0} | all-to-all | bytes 524288 | tf_op jit(solution)/shard_map/all_to_all | solution.py:20
  31.0 1.4 reshape.167
  32.5 3.6 %copy.63 = bf16[2,16,32,128]{3,1,2,0:T(8,128)(2,1)} copy(bf16[2,16,32,128]{1,0,3,2:T(2,128)(2,1)S(1)} %bitcast.67) | data formatting | bytes 524288 | tf_op jit(solution)/shard_map/all_to_all | solution.py:20
  37.3 0.8 scatter_custom_fusion
  38.4 12.5 %all-gather.5.cloned.1.call-done = bf16[2,2,256,512]{3,2,1,0:T(8,128)(2,1)} async-done(((bf16[2,2,256,128]{3,2,1,0:T(8,128)(2,1)}), bf16[2,2,256,512]{3,2,1,0:T(8,128)(2,1)}) %all-gather.5.cloned.1.call-update) | async-done | bytes 1048592 | tf_op jit(solution)/shard_map/all_gather | solution.py:22
  50.9 1.3 slice_negate_fusion
  52.3 1.0 copy.50
  53.3 1.2 pad_maximum_fusion.1
  54.6 0.8 copy.54
  56.6 47.4 %all-gather.3.cloned.1.call-done = bf16[2,2,256,1024]{3,2,1,0:T(8,128)(2,1)} async-done(((bf16[2,2,256,128]{3,2,1,0:T(8,128)(2,1)}), bf16[2,2,256,1024]{3,2,1,0:T(8,128)(2,1)}) %all-gather.3.cloned.1.call-update) | async-done | bytes 2097168 | tf_op jit(solution)/shard_map/all_gather | solution.py:40
  104.0 100.7 %while.19 = (s32[]{:T(128)}, f32[8,8,4,256]{3,0,1,2:T(8,128)S(1)}, s32[]{:T(128)}, s32[]{:T(128)}, s32[8,4]{1,0:T(8,128)S(1)}, /*index=5*/bf16[2,2,256,1024]{3,2...) while((s32[]{:T(128)}, f32[8,8,4,256]{3,0,1,2:T(8,128)S(1)}, ...), condition=%wide.region_2.3_spmd.clone, body=%wide.region_1.2_spmd.clone.sunk | while | flops 1082400768 | bytes 8094242 | solution.py:65
  104.1 1.0 constant_dynamic-slice_fusion.8
  106.0 10.4 %fusion.26 = f32[4,2,2,256,1]{3,0,4,2,1:T(4,128)S(1)} fusion(s32[128,128]{1,0:T(8,128)S(1)} %get-tuple-element.514, f32[4,2,2,128,128]{4,3,0,1,2:T(8,128)S(1)} %pad_maximum_fusion.3), kind=kOutput, calls=%fused_computation.3.clone.1 | convolution fusion | flops 813694976 | bytes 1130496 | tf_op jit(solution)/shard_map/while/body/eval_jaxpr/qcpab,abs->qcps/dot_general | solution.py:52
  116.7 1.0 constant_dynamic-slice_fusion.8
  118.6 10.4 %fusion.26 = f32[4,2,2,256,1]{3,0,4,2,1:T(4,128)S(1)} fusion(s32[128,128]{1,0:T(8,128)S(1)} %get-tuple-element.514, f32[4,2,2,128,128]{4,3,0,1,2:T(8,128)S(1)} %pad_maximum_fusion.3), kind=kOutput, calls=%fused_computation.3.clone.1 | convolution fusion | flops 813694976 | bytes 1130496 | tf_op jit(solution)/shard_map/while/body/eval_jaxpr/qcpab,abs->qcps/dot_general | solution.py:52
  129.3 1.0 constant_dynamic-slice_fusion.8
  131.1 10.4 %fusion.26 = f32[4,2,2,256,1]{3,0,4,2,1:T(4,128)S(1)} fusion(s32[128,128]{1,0:T(8,128)S(1)} %get-tuple-element.514, f32[4,2,2,128,128]{4,3,0,1,2:T(8,128)S(1)} %pad_maximum_fusion.3), kind=kOutput, calls=%fused_computation.3.clone.1 | convolution fusion | flops 813694976 | bytes 1130496 | tf_op jit(solution)/shard_map/while/body/eval_jaxpr/qcpab,abs->qcps/dot_general | solution.py:52
  141.9 1.0 constant_dynamic-slice_fusion.8
  143.7 10.4 %fusion.26 = f32[4,2,2,256,1]{3,0,4,2,1:T(4,128)S(1)} fusion(s32[128,128]{1,0:T(8,128)S(1)} %get-tuple-element.514, f32[4,2,2,128,128]{4,3,0,1,2:T(8,128)S(1)} %pad_maximum_fusion.3), kind=kOutput, calls=%fused_computation.3.clone.1 | convolution fusion | flops 813694976 | bytes 1130496 | tf_op jit(solution)/shard_map/while/body/eval_jaxpr/qcpab,abs->qcps/dot_general | solution.py:52
  154.4 1.0 constant_dynamic-slice_fusion.8
  156.3 10.4 %fusion.26 = f32[4,2,2,256,1]{3,0,4,2,1:T(4,128)S(1)} fusion(s32[128,128]{1,0:T(8,128)S(1)} %get-tuple-element.514, f32[4,2,2,128,128]{4,3,0,1,2:T(8,128)S(1)} %pad_maximum_fusion.3), kind=kOutput, calls=%fused_computation.3.clone.1 | convolution fusion | flops 813694976 | bytes 1130496 | tf_op jit(solution)/shard_map/while/body/eval_jaxpr/qcpab,abs->qcps/dot_general | solution.py:52
  167.0 1.0 constant_dynamic-slice_fusion.8
  168.9 10.4 %fusion.26 = f32[4,2,2,256,1]{3,0,4,2,1:T(4,128)S(1)} fusion(s32[128,128]{1,0:T(8,128)S(1)} %get-tuple-element.514, f32[4,2,2,128,128]{4,3,0,1,2:T(8,128)S(1)} %pad_maximum_fusion.3), kind=kOutput, calls=%fused_computation.3.clone.1 | convolution fusion | flops 813694976 | bytes 1130496 | tf_op jit(solution)/shard_map/while/body/eval_jaxpr/qcpab,abs->qcps/dot_general | solution.py:52
  179.6 1.0 constant_dynamic-slice_fusion.8
  181.5 10.4 %fusion.26 = f32[4,2,2,256,1]{3,0,4,2,1:T(4,128)S(1)} fusion(s32[128,128]{1,0:T(8,128)S(1)} %get-tuple-element.514, f32[4,2,2,128,128]{4,3,0,1,2:T(8,128)S(1)} %pad_maximum_fusion.3), kind=kOutput, calls=%fused_computation.3.clone.1 | convolution fusion | flops 813694976 | bytes 1130496 | tf_op jit(solution)/shard_map/while/body/eval_jaxpr/qcpab,abs->qcps/dot_general | solution.py:52
  192.2 1.0 constant_dynamic-slice_fusion.8
  194.0 10.4 %fusion.26 = f32[4,2,2,256,1]{3,0,4,2,1:T(4,128)S(1)} fusion(s32[128,128]{1,0:T(8,128)S(1)} %get-tuple-element.514, f32[4,2,2,128,128]{4,3,0,1,2:T(8,128)S(1)} %pad_maximum_fusion.3), kind=kOutput, calls=%fused_computation.3.clone.1 | convolution fusion | flops 813694976 | bytes 1130496 | tf_op jit(solution)/shard_map/while/body/eval_jaxpr/qcpab,abs->qcps/dot_general | solution.py:52
  205.6 0.8 broadcast_select_fusion
  206.5 123.3 %all-reduce.3.cloned.1.call-done = f32[64,4,255]{2,1,0:T(4,128)} async-done(((f32[64,4,255]{2,1,0:T(4,128)}), f32[64,4,255]{2,1,0:T(4,128)}) %all-reduce.3.cloned.1.call-update) | async-done | bytes 261136
  329.8 1.3 dynamic-slice_multiply_fusion
  (105 shorter events, 12.3 us)
Async XLA Ops:
  6.5 44.3 %all-gather.5.cloned.1.call-start = ((), (), s32[]{:S(2)}) async-start(), calls=%async_computation.2 | async-start | bytes 1310720 | tf_op jit(solution)/shard_map/all_gather | solution.py:22
  31.0 5.9 %copy-start.1 = (s32[32,32]{1,0:T(8,128)S(1)}, s32[32,32]{1,0:T(8,128)}, u32[]{:S(2)}) copy-start(s32[32,32]{1,0:T(8,128)} %param.6) | copy-start | bytes 12292
  32.5 4.8 %copy-start.2 = (s32[64]{0:T(128)S(1)}, s32[64]{0:T(128)}, u32[]{:S(2)}) copy-start(s32[64]{0:T(128)} %param.7) | copy-start | bytes 772
  36.1 67.9 %all-gather.3.cloned.1.call-start = ((), (), s32[]{:S(2)}) async-start(), calls=%async_computation.1 | async-start | bytes 2359296 | tf_op jit(solution)/shard_map/all_gather | solution.py:40
  36.8 292.9 %all-reduce.3.cloned.1.call-start = ((), (), s32[]{:S(2)}) async-start(), calls=%async_computation.3 | async-start | bytes 524288
  53.3 2.1 copy-start
Sparse Core Ops, SparseCore 0:
  36.2 14.5 all-gather.4
  52.9 51.0 all-gather.2
  206.6 123.1 all-reduce.2
where the time goes:
time: 338 us
  waiting for transfers between devices  184 us (54%)
  matrix products  88.2 us (26%)
  local copies, waits for them, and re-layouts  27.1 us (8%)
  blocking collectives  17.8 us (5%)
  between operations  13.3 us (4%)
  other arithmetic  6.33 us (2%)
    unnamed x4, waiting for transfers between devices  124 us
    dot_general x8, matrix products, one_row(): folded = jnp.einsum('qcpab,abs->qcps', gram, fold_table, precision=highest)  83.3 us
    all_gather x1, waiting for transfers between devices, per_device(): piece = lax.all_gather(local_volts, 'col', axis=3, tiled=True)  47.4 us
    all_to_all x1, blocking collectives, per_device(): lax.all_to_all(volts, ('row', 'col'), split_axis=2, concat_axis=1, tiled=...  17.8 us
    all_gather x1, waiting for transfers between devices, per_device(): column_side = lax.all_gather(local_volts, 'row', axis=3, tiled=True)  12.5 us
    unnamed x13, local copies, waits for them, and re-layouts  9.92 us
    dynamic_slice x16, local copies, waits for them, and re-layouts, one_row(): lax.dynamic_slice_in_dim(piece, offset * GRID_COLUMNS, GRID_COLUMNS, 3)  8.98 us
  transfers between devices with their start and end apart: 3, of which 3 were waited for; matrix products, arithmetic and copies ran while one was open for 2% of the time, Pallas kernels for 0%

commit v1 on v0

v1 whole, which is shorter than its diff:
```python
import functools

import jax
import jax.numpy as jnp
from jax import lax
from jax.experimental import pallas as pl
from jax.experimental.pallas import tpu as pltpu
from jax.sharding import PartitionSpec as P

GRID_COLUMNS = 128
CHAN = 2
TIME_SAMPLES = 256
DEPTH = 256
MESH = pl.DeviceIdType.MESH


def iota(shape, dim):
    return lax.broadcasted_iota(jnp.int32, shape, dim)


def one_hot(condition):
    return jnp.where(condition, 1.0, 0.0).astype(jnp.bfloat16)


def dot(a, b, contract=((1,), (0,))):
    return lax.dot_general(a, b, (contract, ((), ())), preferred_element_type=jnp.float32)


def split3(x):
    high = x.astype(jnp.bfloat16)
    rest = x - high.astype(jnp.float32)
    middle = rest.astype(jnp.bfloat16)
    low = (rest - middle.astype(jnp.float32)).astype(jnp.bfloat16)
    return high, middle, low


def kernel(row_count, col_count, volts_ref, pattern_ref, owner_ref, out_ref,
           rhs_ref, lhs_ref, mask_ref, acc_ref, send_ref, recv_ref, send_sem, recv_sem):
    device_count = row_count * col_count
    grid_rows = pattern_ref.shape[0]
    samples = volts_ref.shape[1]
    unit = 2 * samples
    total = grid_rows * unit
    width = GRID_COLUMNS
    stack_count = owner_ref.shape[1]
    mask_width = mask_ref.shape[1]
    me = lax.axis_index("row") * col_count + lax.axis_index("col")

    barrier = pltpu.get_barrier_semaphore()

    def greet(step, carry):
        other = lax.rem(me + step, device_count)
        pl.semaphore_signal(barrier, inc=1, device_id=(other // col_count, lax.rem(other, col_count)),
                            device_id_type=MESH)
        return carry

    lax.fori_loop(1, device_count, greet, 0)

    store = rhs_ref.dtype
    for p in range(grid_rows):
        real = volts_ref[0, :, p * width:(p + 1) * width].astype(store)
        imag = volts_ref[1, :, p * width:(p + 1) * width].astype(store)
        start = p * unit
        rhs_ref[start:start + samples, :width] = real
        rhs_ref[start + samples:start + unit, :width] = imag
        rhs_ref[start:start + samples, width:] = -imag
        rhs_ref[start + samples:start + unit, width:] = real
    rhs_ref[total:, :] = jnp.zeros((DEPTH, 2 * width), store)

    flip = one_hot(iota((width, width), 0) + iota((width, width), 1) == width - 1)
    for block in range(total // DEPTH):
        rows = rhs_ref[block * DEPTH:(block + 1) * DEPTH, :width].astype(jnp.bfloat16)
        lhs_ref[:, block * DEPTH:(block + 1) * DEPTH] = dot(flip, rows, ((1,), (1,))).astype(jnp.bfloat16)

    valid = one_hot(pattern_ref[...] >= 0)
    flip_rows = one_hot(iota((grid_rows, grid_rows), 0) + iota((grid_rows, grid_rows), 1) == grid_rows - 1)
    widen = one_hot(iota((grid_rows, mask_width), 0) == iota((grid_rows, mask_width), 1))
    spread = one_hot(iota((grid_rows, total), 1) // unit == grid_rows - 1 - iota((grid_rows, total), 0))
    count = None
    for sign, contract in enumerate((((1,), (0,)), ((1,), (1,)))):
        turned = dot(flip_rows, valid, contract).astype(jnp.bfloat16)
        skewed = pltpu.roll(dot(turned, widen), 0, 1, stride=1, stride_axis=0).T.astype(jnp.bfloat16)
        mask_ref[sign] = dot(skewed, spread)
        if sign == 0:
            count = dot(skewed, jnp.ones((grid_rows, width), jnp.bfloat16))[:stack_count]

    no_pairs = jnp.zeros((8, 2 * width), jnp.float32)
    for part in range(2):
        acc_ref[part, grid_rows - 1] = no_pairs
        acc_ref[part, stack_count - 1] = no_pairs

    unwrapped = iota((width, width), 1) >= iota((width, width), 0)

    def one_difference(depth, d, carry):
        row = pl.ds(grid_rows - 1 + d, 1)
        left = lhs_ref[:, :depth]
        left = jnp.concatenate(
            [left * mask_ref[sign, row, :depth].astype(jnp.bfloat16) for sign in range(2)], axis=0
        )
        right = rhs_ref[pl.ds(pl.multiple_of(d * unit, unit), depth), :].astype(jnp.bfloat16)
        gram = dot(left, right)
        for sign in range(2):
            k = grid_rows - 1 + d if sign == 0 else grid_rows - 1 - d
            for part in range(2):
                tile = gram[sign * width:(sign + 1) * width, part * width:(part + 1) * width]
                tile = pltpu.roll(tile, 0, 1, stride=1, stride_axis=0)
                first = jnp.where(unwrapped, tile, 0.0).reshape(width // 8, 8, width)
                second = jnp.where(unwrapped, 0.0, tile).reshape(width // 8, 8, width)
                acc_ref[part, k, :, :width] = jnp.sum(first, axis=0)
                acc_ref[part, k, :, width:] = jnp.sum(second, axis=0)
        return carry

    per_block = DEPTH // unit
    for blocks in range(total // DEPTH, 0, -1):
        begin = max(1, grid_rows - blocks * per_block)
        end = grid_rows - (blocks - 1) * per_block
        lax.fori_loop(begin, end, functools.partial(one_difference, blocks * DEPTH), 0)

    lanes = 2 * width
    reverse = one_hot(iota((lanes, lanes), 0) + iota((lanes, lanes), 1) == lanes - 2)
    offsets = jnp.abs(iota((stack_count, lanes), 1) - (width - 1)).astype(jnp.float32)
    pairs = jnp.concatenate([count, count], axis=1) * (width - offsets)
    scale = 1.0 / jnp.sqrt(2.0 * TIME_SAMPLES * jnp.maximum(pairs, 1.0))
    parts = []
    for part in range(2):
        folded = jnp.sum(acc_ref[part], axis=1)
        behind = sum(dot(piece, reverse) for piece in split3(folded[:grid_rows]))
        if part == 1:
            behind = -behind
        parts.append(jnp.concatenate([behind, folded[grid_rows:]], axis=0) * scale)
    stacked = jnp.concatenate(parts, axis=1)

    send_rows = device_count * 8
    index = iota((send_rows, stack_count), 0)
    wanted = one_hot(index // 4 == owner_ref[...])
    picked = sum(dot(wanted, piece) for piece in split3(stacked))
    quarter = iota((send_rows, width), 0) % 4
    blocks = picked[:, 3 * width:]
    for m in range(3):
        blocks = jnp.where(quarter == m, picked[:, m * width:(m + 1) * width], blocks)
    send_ref[...] = blocks.reshape(device_count, 8, width)

    pl.semaphore_wait(barrier, device_count - 1)

    def send(step, carry):
        other = lax.rem(me + step, device_count)
        pltpu.make_async_remote_copy(
            src_ref=send_ref.at[other], dst_ref=recv_ref.at[me], send_sem=send_sem, recv_sem=recv_sem,
            device_id=(other // col_count, lax.rem(other, col_count)), device_id_type=MESH,
        ).start()
        return carry

    lax.fori_loop(1, device_count, send, 0)
    recv_ref[me] = send_ref[me]
    others = pl.ds(0, device_count - 1)
    pltpu.make_async_copy(recv_ref.at[others], recv_ref.at[others], recv_sem).wait()
    half = device_count // CHAN
    for chan in range(CHAN):
        owned = jnp.sum(recv_ref[chan * half:(chan + 1) * half], axis=0)
        for slot in range(2):
            for part in range(2):
                line = slot * 4 + part * 2
                out_ref[slot, chan * 2 + part, :width] = owned[line]
                out_ref[slot, chan * 2 + part, width:] = owned[line + 1, :width - 1]
    pltpu.make_async_copy(send_ref.at[others], send_ref.at[others], send_sem).wait()


def per_device(volts, pattern, owner_slot):
    row_count = lax.axis_size("row")
    col_count = lax.axis_size("col")
    device_count = row_count * col_count
    grid_rows = pattern.shape[0]
    stack_count = owner_slot.shape[0]
    samples = volts.shape[1]
    total = grid_rows * 2 * samples
    store = jnp.bfloat16 if samples % 16 == 0 else jnp.float32
    mask_width = -(-stack_count // 128) * 128
    vmem = pl.BlockSpec(memory_space=pltpu.VMEM)
    return pl.pallas_call(
        functools.partial(kernel, row_count, col_count),
        out_shape=jax.ShapeDtypeStruct(
            (stack_count // device_count, 2 * CHAN, 2 * GRID_COLUMNS - 1), jnp.float32),
        in_specs=[vmem] * 3,
        out_specs=vmem,
        scratch_shapes=[
            pltpu.VMEM((total + DEPTH, 2 * GRID_COLUMNS), store),
            pltpu.VMEM((GRID_COLUMNS, total), jnp.bfloat16),
            pltpu.VMEM((2, mask_width, total), jnp.float32),
            pltpu.VMEM((2, stack_count, 8, 2 * GRID_COLUMNS), jnp.float32),
            pltpu.VMEM((device_count, 8, GRID_COLUMNS), jnp.float32),
            pltpu.VMEM((device_count, 8, GRID_COLUMNS), jnp.float32),
            pltpu.SemaphoreType.DMA,
            pltpu.SemaphoreType.DMA,
        ],
        compiler_params=pltpu.CompilerParams(
            collective_id=0, has_side_effects=True, vmem_limit_bytes=48 * 1024 * 1024),
        cost_estimate=pl.CostEstimate(flops=2 * 256 * 256 * 19456, bytes_accessed=1 << 20, transcendentals=0),
    )(volts, pattern, owner_slot.reshape(1, stack_count))


def solution(mesh):
    return jax.shard_map(
        per_device,
        mesh=mesh,
        in_specs=(P(None, ("row", "col"), None), P(), P()),
        out_specs=P(("row", "col"), None, None),
        check_vma=False,
    )
```

time: 338 us -> 24.8 us (0.07)
  waiting for transfers between devices: 184 us -> 0 us
  matrix products: 88.2 us -> 0 us
  local copies, waits for them, and re-layouts: 27.1 us -> 2.92 us
  Pallas kernels: 0 us -> 21.6 us
  blocking collectives: 17.8 us -> 0 us
  between operations: 13.3 us -> 0.01 us
  other arithmetic: 6.33 us -> 0 us
    unnamed x4 -> x0, waiting for transfers between devices: 124 us -> none
    dot_general x24 -> x0, matrix products: 88.2 us -> none  [the longest x8 83.3 us: one_row(): folded = jnp.einsum('qcpab,abs->qcps', gram, fold_table, precision=highest)]
    all_gather x2 -> x0, waiting for transfers between devices: 59.8 us -> none  [the longest x1 47.4 us: per_device(): piece = lax.all_gather(local_volts, 'col', axis=3, tiled=True)]
    pallas_call x0 -> x1, Pallas kernels: none -> 21.6 us  [per_device(): pl.pallas_call(functools.partial(kernel, row_count, col_count), out_shape...]
    all_to_all x1 -> x0, blocking collectives: 17.8 us -> none  [per_device(): lax.all_to_all(volts, ('row', 'col'), split_axis=2, concat_axis=1, tiled=...]
    dynamic_slice x28 -> x0, local copies, waits for them, and re-layouts: 9.4 us -> none  [the longest x16 8.98 us: one_row(): lax.dynamic_slice_in_dim(piece, offset * GRID_COLUMNS, GRID_COLUMNS, 3)]
    unnamed x13 -> x7, local copies, waits for them, and re-layouts: 9.92 us -> 2.92 us
    all_to_all x1 -> x0, local copies, waits for them, and re-layouts: 3.6 us -> none  [per_device(): lax.all_to_all(volts, ('row', 'col'), split_axis=2, concat_axis=1, tiled=...]
  transfers between devices with their start and end apart: 3 -> 0, of which waited for: 3 -> 0; matrix products, arithmetic and copies ran while one was open for 2% -> 0% of each run, Pallas kernels for 0% -> 0%
where the time goes in v1:
time: 24.8 us; the launch traced here: 24.6 us
  Pallas kernels  21.6 us (87%)
  local copies, waits for them, and re-layouts  2.92 us (12%)
    pallas_call x1, Pallas kernels, per_device(): pl.pallas_call(functools.partial(kernel, row_count, col_count), out_shape...  21.6 us
    unnamed x7, local copies, waits for them, and re-layouts  2.92 us

profile of v1, /device:TPU:0, one launch (start us, length us, event | category | flops | bytes accessed | tf_op | source)
XLA Modules:
  0.0 24.6 jit_solution(15147983569733058076)
XLA Ops:
  0.0 0.0 copy-start.2
  0.0 0.7 %copy-done.2 = s32[64]{0:T(128)S(1)} copy-done((s32[64]{0:T(128)S(1)}, s32[64]{0:T(128)}, u32[]{:S(2)}) %copy-start.2) | copy-done | bytes 280
  0.7 0.0 copy-start
  0.7 0.9 %copy-done = bf16[2,16,4096]{2,1,0:T(8,128)(2,1)S(1)} copy-done((bf16[2,16,4096]{2,1,0:T(8,128)(2,1)S(1)}, bf16[2,16,4096]{2,1,0:T(8,128)(2,1)}, u32[]{:S(2)}) %copy-start) | copy-done | bytes 262168
  1.6 0.0 copy-start.1
  1.6 0.7 %copy-done.1 = s32[32,32]{1,0:T(8,128)S(1)} copy-done((s32[32,32]{1,0:T(8,128)S(1)}, s32[32,32]{1,0:T(8,128)}, u32[]{:S(2)}) %copy-start.1) | copy-done | bytes 4120
  2.3 21.6 %shard_map.37 = f32[2,4,255]{2,1,0:T(4,128)S(1)} custom-call(bf16[2,16,4096]{2,1,0:T(8,128)(2,1)S(1)} %copy-done, s32[32,32]{1,0:T(8,128)S(1)} %copy-done.1, s32[1,64]{1,0:T(1,128)S(1)} %bitcast.1), custom_call_target="tpu_custom_call" | custom-call | flops 2550136832 | bytes 1048576 | tf_op jit(solution)/shard_map/pallas_call | solution.py:179
  24.0 0.6 %copy.5 = f32[2,4,255]{2,1,0:T(4,128)} copy(f32[2,4,255]{2,1,0:T(4,128)S(1)} %shard_map.37) | data formatting | bytes 16320
Async XLA Ops:
  0.0 0.7 %copy-start.2 = (s32[64]{0:T(128)S(1)}, s32[64]{0:T(128)}, u32[]{:S(2)}) copy-start(s32[64]{0:T(128)} %param.5) | copy-start | bytes 772
  0.7 0.9 %copy-start = (bf16[2,16,4096]{2,1,0:T(8,128)(2,1)S(1)}, bf16[2,16,4096]{2,1,0:T(8,128)(2,1)}, u32[]{:S(2)}) copy-start(bf16[2,16,4096]{2,1,0:T(8,128)(2,1)} %volts_ref.1) | copy-start | bytes 786436
  1.6 0.7 %copy-start.1 = (s32[32,32]{1,0:T(8,128)S(1)}, s32[32,32]{1,0:T(8,128)}, u32[]{:S(2)}) copy-start(s32[32,32]{1,0:T(8,128)} %pattern_ref.1) | copy-start | bytes 12292

commit v2 on v1

v2 whole, which is shorter than its diff:
```python
import functools

import jax
import jax.numpy as jnp
from jax import lax
from jax.experimental import pallas as pl
from jax.experimental.pallas import tpu as pltpu
from jax.sharding import PartitionSpec as P

GRID_COLUMNS = 128
CHAN = 2
TIME_SAMPLES = 256
DEPTH = 256
UNROLL = 4
MESH = pl.DeviceIdType.MESH


def iota(shape, dim):
    return lax.broadcasted_iota(jnp.int32, shape, dim)


def one_hot(condition):
    return jnp.where(condition, 1.0, 0.0).astype(jnp.bfloat16)


def dot(a, b, contract=((1,), (0,))):
    return lax.dot_general(a, b, (contract, ((), ())), preferred_element_type=jnp.float32)


def split3(x):
    high = x.astype(jnp.bfloat16)
    rest = x - high.astype(jnp.float32)
    middle = rest.astype(jnp.bfloat16)
    low = (rest - middle.astype(jnp.float32)).astype(jnp.bfloat16)
    return high, middle, low


def kernel(row_count, col_count, volts_hbm, pattern_hbm, owner_hbm, out_ref,
           volts_ref, pattern_ref, owner_ref, rhs_ref, lhs_ref, mask_ref, scale_ref, wanted_ref, sum_ref,
           send_ref, recv_ref, load_sems, send_sem, recv_sem):
    device_count = row_count * col_count
    grid_rows = pattern_ref.shape[0]
    samples = volts_ref.shape[1]
    unit = 2 * samples
    total = grid_rows * unit
    width = GRID_COLUMNS
    lanes = 2 * width
    stack_count = owner_ref.shape[1]
    mask_width = -(-stack_count // 128) * 128
    me = lax.axis_index("row") * col_count + lax.axis_index("col")

    def place(device):
        return (device // col_count, lax.rem(device, col_count))

    loads = [
        pltpu.make_async_copy(source, target, load_sems.at[n])
        for n, (source, target) in enumerate(
            ((pattern_hbm, pattern_ref), (owner_hbm, owner_ref), (volts_hbm, volts_ref)))
    ]
    for load in loads:
        load.start()

    barrier = pltpu.get_barrier_semaphore()

    def greet(step, carry):
        other = lax.rem(me + step, device_count)
        pl.semaphore_signal(barrier, inc=1, device_id=place(other), device_id_type=MESH)
        return carry

    lax.fori_loop(1, device_count, greet, 0)

    loads[0].wait()
    valid = one_hot(pattern_ref[...] >= 0)
    flip_rows = one_hot(iota((grid_rows, grid_rows), 0) + iota((grid_rows, grid_rows), 1) == grid_rows - 1)
    widen = one_hot(iota((grid_rows, mask_width), 0) == iota((grid_rows, mask_width), 1))
    spread = one_hot(iota((grid_rows, total), 1) // unit == grid_rows - 1 - iota((grid_rows, total), 0))
    for sign, contract in enumerate((((1,), (0,)), ((1,), (1,)))):
        turned = dot(dot(flip_rows, valid, contract).astype(jnp.bfloat16), widen)
        skewed = pltpu.roll(turned, mask_width - (grid_rows - 1), 1, stride=1, stride_axis=0)
        mask_ref[sign] = dot(skewed.T.astype(jnp.bfloat16)[:grid_rows], spread)
        if sign == 0:
            by_stack = pltpu.roll(turned, 0, 1, stride=1, stride_axis=0).T.astype(jnp.bfloat16)
            count = dot(by_stack, jnp.ones((grid_rows, lanes), jnp.bfloat16))[:stack_count]
            offsets = jnp.abs(iota((stack_count, lanes), 1) - (width - 1)).astype(jnp.float32)
            pairs = jnp.maximum(count * (width - offsets), 1.0)
            scale_ref[...] = 1.0 / jnp.sqrt(2.0 * TIME_SAMPLES * pairs)

    loads[1].wait()
    send_rows = device_count * 8
    owner = owner_ref[...]
    owner = jnp.concatenate([owner, owner, owner], axis=1)
    wanted_ref[...] = one_hot(iota((send_rows, 3 * stack_count), 0) // 4 == owner)

    rhs_ref[total:, :] = jnp.zeros((DEPTH, lanes), rhs_ref.dtype)
    sum_ref[:, stack_count - 8:, :] = jnp.zeros((4, 8, width), jnp.float32)

    loads[2].wait()
    store = rhs_ref.dtype
    for p in range(grid_rows):
        real = volts_ref[0, :, p * width:(p + 1) * width].astype(store)
        imag = volts_ref[1, :, p * width:(p + 1) * width].astype(store)
        start = p * unit
        rhs_ref[start:start + samples, :width] = real
        rhs_ref[start + samples:start + unit, :width] = imag
        rhs_ref[start:start + samples, width:] = -imag
        rhs_ref[start + samples:start + unit, width:] = real

    flip = one_hot(iota((width, width), 0) + iota((width, width), 1) == width - 1)
    for block in range(total // DEPTH):
        rows = rhs_ref[block * DEPTH:(block + 1) * DEPTH, :width].astype(jnp.bfloat16)
        lhs_ref[:, block * DEPTH:(block + 1) * DEPTH] = dot(flip, rows, ((1,), (1,))).astype(jnp.bfloat16)

    unwrapped = iota((width, width), 1) >= iota((width, width), 0)

    def one_difference(depth, d, carry):
        left = lhs_ref[:, :depth]
        left = jnp.concatenate(
            [left * mask_ref[sign, pl.ds(d, 1), :depth].astype(jnp.bfloat16) for sign in range(2)], axis=0
        )
        right = rhs_ref[pl.ds(pl.multiple_of(d * unit, unit), depth), :].astype(jnp.bfloat16)
        gram = dot(left, right)
        for sign in range(2):
            k = grid_rows - 1 + d if sign == 0 else grid_rows - 1 - d
            for part in range(2):
                tile = gram[sign * width:(sign + 1) * width, part * width:(part + 1) * width]
                tile = pltpu.roll(tile, 0, 1, stride=1, stride_axis=0)
                first = jnp.where(unwrapped, tile, 0.0)
                second = jnp.where(unwrapped, 0.0, tile)
                sum_ref[2 * part, pl.ds(k, 1), :] = jnp.sum(first, axis=0, keepdims=True)
                sum_ref[2 * part + 1, pl.ds(k, 1), :] = jnp.sum(second, axis=0, keepdims=True)
        return carry

    per_block = DEPTH // unit
    for blocks in range(total // DEPTH, 0, -1):
        lax.fori_loop(
            grid_rows - blocks * per_block, grid_rows - (blocks - 1) * per_block,
            functools.partial(one_difference, blocks * DEPTH), 0, unroll=UNROLL)

    reverse = one_hot(iota((lanes, lanes), 0) + iota((lanes, lanes), 1) == lanes - 2)
    folded = [jnp.concatenate([sum_ref[2 * part], sum_ref[2 * part + 1]], axis=1) for part in range(2)]
    behind = jnp.concatenate([folded[part][:grid_rows] for part in range(2)], axis=0)
    behind = dot(jnp.concatenate(split3(behind), axis=0), reverse)
    behind = sum(behind[n * 2 * grid_rows:(n + 1) * 2 * grid_rows] for n in range(3))
    scale = scale_ref[...]
    real = jnp.concatenate([behind[:grid_rows], folded[0][grid_rows:]], axis=0) * scale
    imag = jnp.concatenate([-behind[grid_rows:], folded[1][grid_rows:]], axis=0) * scale
    stacked = jnp.concatenate([real, imag], axis=1)
    picked = dot(wanted_ref[...], jnp.concatenate(split3(stacked), axis=0))
    quarter = iota((send_rows, width), 0) % 4
    blocks = picked[:, 3 * width:]
    for m in range(3):
        blocks = jnp.where(quarter == m, picked[:, m * width:(m + 1) * width], blocks)
    send_ref[...] = blocks.reshape(device_count, 8, width)

    pl.semaphore_wait(barrier, device_count - 1)

    def send(step, carry):
        other = lax.rem(me + step, device_count)
        pltpu.make_async_remote_copy(
            src_ref=send_ref.at[other], dst_ref=recv_ref.at[me], send_sem=send_sem, recv_sem=recv_sem,
            device_id=place(other), device_id_type=MESH,
        ).start()
        return carry

    lax.fori_loop(1, device_count, send, 0)
    recv_ref[me] = send_ref[me]
    others = pl.ds(0, device_count - 1)
    pltpu.make_async_copy(recv_ref.at[others], recv_ref.at[others], recv_sem).wait()
    half = device_count // CHAN
    for chan in range(CHAN):
        owned = jnp.sum(recv_ref[chan * half:(chan + 1) * half], axis=0)
        for slot in range(2):
            for part in range(2):
                line = slot * 4 + part * 2
                out_ref[slot, chan * 2 + part, :width] = owned[line]
                out_ref[slot, chan * 2 + part, width:] = owned[line + 1, :width - 1]
    pltpu.make_async_copy(send_ref.at[others], send_ref.at[others], send_sem).wait()


def per_device(volts, pattern, owner_slot):
    row_count = lax.axis_size("row")
    col_count = lax.axis_size("col")
    device_count = row_count * col_count
    grid_rows = pattern.shape[0]
    stack_count = owner_slot.shape[0]
    samples = volts.shape[1]
    total = grid_rows * 2 * samples
    store = jnp.bfloat16 if samples % 16 == 0 else jnp.float32
    vmem = pl.BlockSpec(memory_space=pltpu.VMEM)
    return pl.pallas_call(
        functools.partial(kernel, row_count, col_count),
        out_shape=jax.ShapeDtypeStruct(
            (stack_count // device_count, 2 * CHAN, 2 * GRID_COLUMNS - 1), jnp.float32),
        in_specs=[pl.BlockSpec(memory_space=pltpu.HBM)] * 3,
        out_specs=vmem,
        scratch_shapes=[
            pltpu.VMEM(volts.shape, volts.dtype),
            pltpu.VMEM(pattern.shape, pattern.dtype),
            pltpu.VMEM((1, stack_count), owner_slot.dtype),
            pltpu.VMEM((total + DEPTH, 2 * GRID_COLUMNS), store),
            pltpu.VMEM((GRID_COLUMNS, total), jnp.bfloat16),
            pltpu.VMEM((2, grid_rows, total), jnp.float32),
            pltpu.VMEM((stack_count, 2 * GRID_COLUMNS), jnp.float32),
            pltpu.VMEM((device_count * 8, 3 * stack_count), jnp.bfloat16),
            pltpu.VMEM((4, stack_count, GRID_COLUMNS), jnp.float32),
            pltpu.VMEM((device_count, 8, GRID_COLUMNS), jnp.float32),
            pltpu.VMEM((device_count, 8, GRID_COLUMNS), jnp.float32),
            pltpu.SemaphoreType.DMA((3,)),
            pltpu.SemaphoreType.DMA,
            pltpu.SemaphoreType.DMA,
        ],
        compiler_params=pltpu.CompilerParams(
            collective_id=0, has_side_effects=True, vmem_limit_bytes=48 * 1024 * 1024),
        cost_estimate=pl.CostEstimate(flops=2 * 256 * 256 * 19456, bytes_accessed=1 << 20, transcendentals=0),
    )(volts, pattern, owner_slot.reshape(1, stack_count))


def solution(mesh):
    return jax.shard_map(
        per_device,
        mesh=mesh,
        in_specs=(P(None, ("row", "col"), None), P(), P()),
        out_specs=P(("row", "col"), None, None),
        check_vma=False,
    )
```

time: 24.8 us -> 20 us (0.81)
  Pallas kernels: 21.6 us -> 16.8 us
    pallas_call x1, Pallas kernels: 21.6 us -> 16.8 us  [per_device(): pl.pallas_call(functools.partial(kernel, row_count, col_count), out_shape...]
where the time goes in v2:
time: 20 us; the launch traced here: 19.8 us
  Pallas kernels  16.8 us (84%)
  local copies, waits for them, and re-layouts  2.92 us (15%)
    pallas_call x1, Pallas kernels, per_device(): pl.pallas_call(functools.partial(kernel, row_count, col_count), out_shape...  16.8 us
    unnamed x7, local copies, waits for them, and re-layouts  2.92 us

profile of v2, /device:TPU:0, one launch (start us, length us, event | category | flops | bytes accessed | tf_op | source)
XLA Modules:
  0.0 19.8 jit_solution(17671507862869344044)
XLA Ops:
  0.0 0.0 copy-start.2
  0.0 0.7 %copy-done.2 = s32[64]{0:T(128)S(1)} copy-done((s32[64]{0:T(128)S(1)}, s32[64]{0:T(128)}, u32[]{:S(2)}) %copy-start.2) | copy-done | bytes 280
  0.7 0.0 copy-start
  0.7 0.9 %copy-done = bf16[2,16,4096]{2,1,0:T(8,128)(2,1)S(1)} copy-done((bf16[2,16,4096]{2,1,0:T(8,128)(2,1)S(1)}, bf16[2,16,4096]{2,1,0:T(8,128)(2,1)}, u32[]{:S(2)}) %copy-start) | copy-done | bytes 262168
  1.6 0.0 copy-start.1
  1.6 0.7 %copy-done.1 = s32[32,32]{1,0:T(8,128)S(1)} copy-done((s32[32,32]{1,0:T(8,128)S(1)}, s32[32,32]{1,0:T(8,128)}, u32[]{:S(2)}) %copy-start.1) | copy-done | bytes 4120
  2.3 16.8 %shard_map.37 = f32[2,4,255]{2,1,0:T(4,128)S(1)} custom-call(bf16[2,16,4096]{2,1,0:T(8,128)(2,1)S(1)} %copy-done, s32[32,32]{1,0:T(8,128)S(1)} %copy-done.1, s32[1,64]{1,0:T(1,128)S(1)} %bitcast.1), custom_call_target="tpu_custom_call" | custom-call | flops 2550136832 | bytes 1048576 | tf_op jit(solution)/shard_map/pallas_call | solution.py:190
  19.2 0.6 %copy.5 = f32[2,4,255]{2,1,0:T(4,128)} copy(f32[2,4,255]{2,1,0:T(4,128)S(1)} %shard_map.37) | data formatting | bytes 16320
Async XLA Ops:
  0.0 0.7 %copy-start.2 = (s32[64]{0:T(128)S(1)}, s32[64]{0:T(128)}, u32[]{:S(2)}) copy-start(s32[64]{0:T(128)} %param.5) | copy-start | bytes 772
  0.7 0.9 %copy-start = (bf16[2,16,4096]{2,1,0:T(8,128)(2,1)S(1)}, bf16[2,16,4096]{2,1,0:T(8,128)(2,1)}, u32[]{:S(2)}) copy-start(bf16[2,16,4096]{2,1,0:T(8,128)(2,1)} %volts_hbm.1) | copy-start | bytes 786436
  1.6 0.7 %copy-start.1 = (s32[32,32]{1,0:T(8,128)S(1)}, s32[32,32]{1,0:T(8,128)}, u32[]{:S(2)}) copy-start(s32[32,32]{1,0:T(8,128)} %pattern_hbm.1) | copy-start | bytes 12292

commit v3 on v2

--- a/solution.py
+++ b/solution.py
@@ -11,7 +11,7 @@
 CHAN = 2
 TIME_SAMPLES = 256
 DEPTH = 256
-UNROLL = 4
+UNROLL = 8
 MESH = pl.DeviceIdType.MESH
 
 
@@ -67,7 +67,7 @@
         pl.semaphore_signal(barrier, inc=1, device_id=place(other), device_id_type=MESH)
         return carry
 
-    lax.fori_loop(1, device_count, greet, 0)
+    lax.fori_loop(1, device_count, greet, 0, unroll=device_count <= 32)
 
     loads[0].wait()
     valid = one_hot(pattern_ref[...] >= 0)
@@ -162,7 +162,7 @@
         ).start()
         return carry
 
-    lax.fori_loop(1, device_count, send, 0)
+    lax.fori_loop(1, device_count, send, 0, unroll=device_count <= 32)
     recv_ref[me] = send_ref[me]
     others = pl.ds(0, device_count - 1)
     pltpu.make_async_copy(recv_ref.at[others], recv_ref.at[others], recv_sem).wait()
@@ -210,7 +210,7 @@
             pltpu.SemaphoreType.DMA,
         ],
         compiler_params=pltpu.CompilerParams(
-            collective_id=0, has_side_effects=True, vmem_limit_bytes=48 * 1024 * 1024),
+            collective_id=0, has_side_effects=True, vmem_limit_bytes=60 * 1024 * 1024),
         cost_estimate=pl.CostEstimate(flops=2 * 256 * 256 * 19456, bytes_accessed=1 << 20, transcendentals=0),
     )(volts, pattern, owner_slot.reshape(1, stack_count))
 

time: 20 us -> 16.7 us (0.83)
  Pallas kernels: 16.8 us -> 15.1 us
  local copies, waits for them, and re-layouts: 2.92 us -> 1.3 us
    pallas_call x1, Pallas kernels: 16.8 us -> 15.1 us  [per_device(): pl.pallas_call(functools.partial(kernel, row_count, col_count), out_shape...]
    unnamed x7 -> x1, local copies, waits for them, and re-layouts: 2.92 us -> 1.3 us
where the time goes in v3:
time: 16.7 us; the launch traced here: 16.4 us
  Pallas kernels  15.1 us (90%)
  local copies, waits for them, and re-layouts  1.3 us (8%)
    pallas_call x1, Pallas kernels, per_device(): pl.pallas_call(functools.partial(kernel, row_count, col_count), out_shape...  15.1 us
    unnamed x1, local copies, waits for them, and re-layouts  1.3 us

profile of v3, /device:TPU:0, one launch (start us, length us, event | category | flops | bytes accessed | tf_op | source)
XLA Modules:
  0.0 16.4 jit_solution(12038514247477829863)
XLA Ops:
  0.0 15.1 %shard_map.37 = f32[2,4,255]{2,1,0:T(4,128)} custom-call(bf16[2,16,4096]{2,1,0:T(8,128)(2,1)} %volts_hbm.1, s32[32,32]{1,0:T(8,128)} %pattern_hbm.1, s32[1,64]{1,0:T(1,128)} %bitcast.1), custom_call_target="tpu_custom_call" | custom-call | flops 2550136832 | bytes 1048576 | tf_op jit(solution)/shard_map/pallas_call | solution.py:190
  15.1 1.3 %copy.5 = f32[2,4,255]{2,1,0:T(4,128)} copy(f32[2,4,255]{2,1,0:T(4,128)} %shard_map.37) | data formatting | bytes 16320

commit v4 on v3

--- a/solution.py
+++ b/solution.py
@@ -70,30 +70,25 @@
     lax.fori_loop(1, device_count, greet, 0, unroll=device_count <= 32)
 
     loads[0].wait()
-    valid = one_hot(pattern_ref[...] >= 0)
+    valid = jnp.where(pattern_ref[...] >= 0, 1.0, 0.0)
     flip_rows = one_hot(iota((grid_rows, grid_rows), 0) + iota((grid_rows, grid_rows), 1) == grid_rows - 1)
-    widen = one_hot(iota((grid_rows, mask_width), 0) == iota((grid_rows, mask_width), 1))
+    more = mask_width - grid_rows
+    widened = (
+        jnp.concatenate([valid, jnp.zeros((grid_rows, more), valid.dtype)], axis=1),
+        jnp.concatenate([valid, jnp.zeros((more, grid_rows), valid.dtype)], axis=0),
+    )
     spread = one_hot(iota((grid_rows, total), 1) // unit == grid_rows - 1 - iota((grid_rows, total), 0))
     for sign, contract in enumerate((((1,), (0,)), ((1,), (1,)))):
-        turned = dot(dot(flip_rows, valid, contract).astype(jnp.bfloat16), widen)
+        turned = dot(flip_rows, widened[sign].astype(jnp.bfloat16), contract)
+        if sign == 0:
+            unflipped = turned
         skewed = pltpu.roll(turned, mask_width - (grid_rows - 1), 1, stride=1, stride_axis=0)
         mask_ref[sign] = dot(skewed.T.astype(jnp.bfloat16)[:grid_rows], spread)
-        if sign == 0:
-            by_stack = pltpu.roll(turned, 0, 1, stride=1, stride_axis=0).T.astype(jnp.bfloat16)
-            count = dot(by_stack, jnp.ones((grid_rows, lanes), jnp.bfloat16))[:stack_count]
-            offsets = jnp.abs(iota((stack_count, lanes), 1) - (width - 1)).astype(jnp.float32)
-            pairs = jnp.maximum(count * (width - offsets), 1.0)
-            scale_ref[...] = 1.0 / jnp.sqrt(2.0 * TIME_SAMPLES * pairs)
-
-    loads[1].wait()
-    send_rows = device_count * 8
-    owner = owner_ref[...]
-    owner = jnp.concatenate([owner, owner, owner], axis=1)
-    wanted_ref[...] = one_hot(iota((send_rows, 3 * stack_count), 0) // 4 == owner)
 
     rhs_ref[total:, :] = jnp.zeros((DEPTH, lanes), rhs_ref.dtype)
     sum_ref[:, stack_count - 8:, :] = jnp.zeros((4, 8, width), jnp.float32)
 
+    loads[1].wait()
     loads[2].wait()
     store = rhs_ref.dtype
     for p in range(grid_rows):
@@ -110,13 +105,28 @@
         rows = rhs_ref[block * DEPTH:(block + 1) * DEPTH, :width].astype(jnp.bfloat16)
         lhs_ref[:, block * DEPTH:(block + 1) * DEPTH] = dot(flip, rows, ((1,), (1,))).astype(jnp.bfloat16)
 
+    by_stack = pltpu.roll(unflipped, 0, 1, stride=1, stride_axis=0).T.astype(jnp.bfloat16)
+    count = dot(by_stack, jnp.ones((grid_rows, lanes), jnp.bfloat16))[:stack_count]
+    offsets = jnp.abs(iota((stack_count, lanes), 1) - (width - 1)).astype(jnp.float32)
+    pairs = jnp.maximum(count * (width - offsets), 1.0)
+    scale_ref[...] = 1.0 / jnp.sqrt(2.0 * TIME_SAMPLES * pairs)
+
+    send_rows = device_count * 8
+    owner = owner_ref[...]
+    owner = jnp.concatenate([owner, owner, owner], axis=1)
+    rows = iota((send_rows, 3 * stack_count), 0)
+    slots = lax.rem(me + rows // 8, device_count) * 2 + rows // 4 % 2
+    wanted_ref[...] = one_hot(slots == owner)
+
     unwrapped = iota((width, width), 1) >= iota((width, width), 0)
 
     def one_difference(depth, d, carry):
-        left = lhs_ref[:, :depth]
-        left = jnp.concatenate(
-            [left * mask_ref[sign, pl.ds(d, 1), :depth].astype(jnp.bfloat16) for sign in range(2)], axis=0
-        )
+        left = lhs_ref[:, :depth].reshape(width // 16, 16, depth)
+        masks = [
+            jnp.broadcast_to(mask_ref[sign, pl.ds(d, 1), :depth], (16, depth)).astype(jnp.bfloat16)
+            for sign in range(2)
+        ]
+        left = jnp.concatenate([(left * mask[None]).reshape(width, depth) for mask in masks], axis=0)
         right = rhs_ref[pl.ds(pl.multiple_of(d * unit, unit), depth), :].astype(jnp.bfloat16)
         gram = dot(left, right)
         for sign in range(2):
@@ -145,25 +155,26 @@
     real = jnp.concatenate([behind[:grid_rows], folded[0][grid_rows:]], axis=0) * scale
     imag = jnp.concatenate([-behind[grid_rows:], folded[1][grid_rows:]], axis=0) * scale
     stacked = jnp.concatenate([real, imag], axis=1)
-    picked = dot(wanted_ref[...], jnp.concatenate(split3(stacked), axis=0))
-    quarter = iota((send_rows, width), 0) % 4
-    blocks = picked[:, 3 * width:]
-    for m in range(3):
-        blocks = jnp.where(quarter == m, picked[:, m * width:(m + 1) * width], blocks)
-    send_ref[...] = blocks.reshape(device_count, 8, width)
-
-    pl.semaphore_wait(barrier, device_count - 1)
+    pieces = jnp.concatenate(split3(stacked), axis=0)
 
     def send(step, carry):
-        other = lax.rem(me + step, device_count)
         pltpu.make_async_remote_copy(
-            src_ref=send_ref.at[other], dst_ref=recv_ref.at[me], send_sem=send_sem, recv_sem=recv_sem,
-            device_id=place(other), device_id_type=MESH,
+            src_ref=send_ref.at[step], dst_ref=recv_ref.at[me], send_sem=send_sem, recv_sem=recv_sem,
+            device_id=place(lax.rem(me + step, device_count)), device_id_type=MESH,
         ).start()
         return carry
 
-    lax.fori_loop(1, device_count, send, 0, unroll=device_count <= 32)
-    recv_ref[me] = send_ref[me]
+    group = device_count // 4
+    quarter = iota((group * 8, width), 0) % 4
+    pl.semaphore_wait(barrier, device_count - 1)
+    for first in range(0, device_count, group):
+        picked = dot(wanted_ref[first * 8:(first + group) * 8, :], pieces)
+        blocks = picked[:, 3 * width:]
+        for m in range(3):
+            blocks = jnp.where(quarter == m, picked[:, m * width:(m + 1) * width], blocks)
+        send_ref[first:first + group] = blocks.reshape(group, 8, width)
+        lax.fori_loop(max(first, 1), first + group, send, 0, unroll=device_count <= 32)
+    recv_ref[me] = send_ref[0]
     others = pl.ds(0, device_count - 1)
     pltpu.make_async_copy(recv_ref.at[others], recv_ref.at[others], recv_sem).wait()
     half = device_count // CHAN

time: 16.7 us -> 16.5 us (0.988)
  Pallas kernels: 15.1 us -> 14.8 us
    pallas_call x1, Pallas kernels: 15.1 us -> 14.8 us  [per_device(): pl.pallas_call(functools.partial(kernel, row_count, col_count), out_shape...]
where the time goes in v4:
time: 16.5 us; the launch traced here: 16.2 us
  Pallas kernels  14.8 us (90%)
  local copies, waits for them, and re-layouts  1.3 us (8%)
    pallas_call x1, Pallas kernels, per_device(): pl.pallas_call(functools.partial(kernel, row_count, col_count), out_shape...  14.8 us
    unnamed x1, local copies, waits for them, and re-layouts  1.3 us

profile of v4, /device:TPU:0, one launch (start us, length us, event | category | flops | bytes accessed | tf_op | source)
XLA Modules:
  0.0 16.2 jit_solution(5965609342166451795)
XLA Ops:
  0.0 14.8 %shard_map.37 = f32[2,4,255]{2,1,0:T(4,128)} custom-call(bf16[2,16,4096]{2,1,0:T(8,128)(2,1)} %volts_hbm.1, s32[32,32]{1,0:T(8,128)} %pattern_hbm.1, s32[1,64]{1,0:T(1,128)} %bitcast.1), custom_call_target="tpu_custom_call" | custom-call | flops 2550136832 | bytes 1048576 | tf_op jit(solution)/shard_map/pallas_call | solution.py:201
  14.9 1.3 %copy.5 = f32[2,4,255]{2,1,0:T(4,128)} copy(f32[2,4,255]{2,1,0:T(4,128)} %shard_map.37) | data formatting | bytes 16320

commit v5 on v4

--- a/solution.py
+++ b/solution.py
@@ -221,7 +221,7 @@
             pltpu.SemaphoreType.DMA,
         ],
         compiler_params=pltpu.CompilerParams(
-            collective_id=0, has_side_effects=True, vmem_limit_bytes=60 * 1024 * 1024),
+            collective_id=0, has_side_effects=True, vmem_limit_bytes=55218 * 1024),
         cost_estimate=pl.CostEstimate(flops=2 * 256 * 256 * 19456, bytes_accessed=1 << 20, transcendentals=0),
     )(volts, pattern, owner_slot.reshape(1, stack_count))
 

time: 16.5 us -> 15.8 us (0.958)
  Pallas kernels: 14.8 us -> 14.3 us
    pallas_call x1, Pallas kernels: 14.8 us -> 14.3 us  [per_device(): pl.pallas_call(functools.partial(kernel, row_count, col_count), out_shape...]
    unnamed x1 -> x3, local copies, waits for them, and re-layouts: 1.3 us -> 1.26 us
where the time goes in v5:
time: 15.8 us; the launch traced here: 15.5 us
  Pallas kernels  14.3 us (91%)
  local copies, waits for them, and re-layouts  1.26 us (8%)
    pallas_call x1, Pallas kernels, per_device(): pl.pallas_call(functools.partial(kernel, row_count, col_count), out_shape...  14.3 us
    unnamed x3, local copies, waits for them, and re-layouts  1.26 us

profile of v5, /device:TPU:0, one launch (start us, length us, event | category | flops | bytes accessed | tf_op | source)
XLA Modules:
  0.0 15.5 jit_solution(9651134941689847021)
XLA Ops:
  0.0 0.0 copy-start
  0.0 0.7 %copy-done = s32[64]{0:T(128)S(1)} copy-done((s32[64]{0:T(128)S(1)}, s32[64]{0:T(128)}, u32[]{:S(2)}) %copy-start) | copy-done | bytes 280
  0.7 14.3 %shard_map.37 = f32[2,4,255]{2,1,0:T(4,128)S(1)} custom-call(bf16[2,16,4096]{2,1,0:T(8,128)(2,1)} %volts_hbm.1, s32[32,32]{1,0:T(8,128)} %pattern_hbm.1, s32[1,64]{1,0:T(1,128)S(1)} %bitcast.1), custom_call_target="tpu_custom_call" | custom-call | flops 2550136832 | bytes 1048576 | tf_op jit(solution)/shard_map/pallas_call | solution.py:201
  14.9 0.6 %copy.5 = f32[2,4,255]{2,1,0:T(4,128)} copy(f32[2,4,255]{2,1,0:T(4,128)S(1)} %shard_map.37) | data formatting | bytes 16320
Async XLA Ops:
  0.0 0.7 %copy-start = (s32[64]{0:T(128)S(1)}, s32[64]{0:T(128)}, u32[]{:S(2)}) copy-start(s32[64]{0:T(128)} %param.5) | copy-start | bytes 772

commit v6 on v5

--- a/solution.py
+++ b/solution.py
@@ -87,6 +87,7 @@
 
     rhs_ref[total:, :] = jnp.zeros((DEPTH, lanes), rhs_ref.dtype)
     sum_ref[:, stack_count - 8:, :] = jnp.zeros((4, 8, width), jnp.float32)
+    sum_ref[:, grid_rows - 8:grid_rows, :] = jnp.zeros((4, 8, width), jnp.float32)
 
     loads[1].wait()
     loads[2].wait()
@@ -142,9 +143,11 @@
 
     per_block = DEPTH // unit
     for blocks in range(total // DEPTH, 0, -1):
+        begin = max(1, grid_rows - blocks * per_block)
+        end = grid_rows - (blocks - 1) * per_block
         lax.fori_loop(
-            grid_rows - blocks * per_block, grid_rows - (blocks - 1) * per_block,
-            functools.partial(one_difference, blocks * DEPTH), 0, unroll=UNROLL)
+            begin, end, functools.partial(one_difference, blocks * DEPTH), 0,
+            unroll=end - begin if end - begin <= UNROLL else 1)
 
     reverse = one_hot(iota((lanes, lanes), 0) + iota((lanes, lanes), 1) == lanes - 2)
     folded = [jnp.concatenate([sum_ref[2 * part], sum_ref[2 * part + 1]], axis=1) for part in range(2)]

time: 15.8 us -> 15.6 us (0.987)
  Pallas kernels: 14.3 us -> 14.1 us
    pallas_call x1, Pallas kernels: 14.3 us -> 14.1 us  [per_device(): pl.pallas_call(functools.partial(kernel, row_count, col_count), out_shape...]
where the time goes in v6:
time: 15.6 us; the launch traced here: 15.3 us
  Pallas kernels  14.1 us (90%)
  local copies, waits for them, and re-layouts  1.26 us (8%)
    pallas_call x1, Pallas kernels, per_device(): pl.pallas_call(functools.partial(kernel, row_count, col_count), out_shape...  14.1 us
    unnamed x3, local copies, waits for them, and re-layouts  1.26 us

profile of v6, /device:TPU:0, one launch (start us, length us, event | category | flops | bytes accessed | tf_op | source)
XLA Modules:
  0.0 15.3 jit_solution(10677328472518894684)
XLA Ops:
  0.0 0.0 copy-start
  0.0 0.7 %copy-done = s32[64]{0:T(128)S(1)} copy-done((s32[64]{0:T(128)S(1)}, s32[64]{0:T(128)}, u32[]{:S(2)}) %copy-start) | copy-done | bytes 280
  0.7 14.1 %shard_map.37 = f32[2,4,255]{2,1,0:T(4,128)S(1)} custom-call(bf16[2,16,4096]{2,1,0:T(8,128)(2,1)} %volts_hbm.1, s32[32,32]{1,0:T(8,128)} %pattern_hbm.1, s32[1,64]{1,0:T(1,128)S(1)} %bitcast.1), custom_call_target="tpu_custom_call" | custom-call | flops 2550136832 | bytes 1048576 | tf_op jit(solution)/shard_map/pallas_call | solution.py:204
  14.7 0.6 %copy.5 = f32[2,4,255]{2,1,0:T(4,128)} copy(f32[2,4,255]{2,1,0:T(4,128)S(1)} %shard_map.37) | data formatting | bytes 16320
Async XLA Ops:
  0.0 0.7 %copy-start = (s32[64]{0:T(128)S(1)}, s32[64]{0:T(128)}, u32[]{:S(2)}) copy-start(s32[64]{0:T(128)} %param.5) | copy-start | bytes 772
